TPU v7x, 128 devices: a whole 4x4x4 slice. The times are simulated.
128 devices in a mesh: dp: 8 (over y, x_lo), feat: 16 (over z, x_hi, core).
Axes of the slice: x: 4 (x_hi: 2, x_lo: 2; x = x_hi * 2 + x_lo), y: 4, z: 4, core: 2. Of those that a mesh axis runs over, the one named last changes fastest.
Arguments:
- fisher: bfloat16 [4096, 32768], P('dp', 'feat'), may hold values from -0.03125 to 0.03125
- sample_ids: int32 [4096], P('dp'), may hold values from 0 to 511
- labels: int32 [4096, 604], P('dp'), may hold values 0 or 1
- weights: bfloat16 [32768, 604], P('feat'), may hold values from -26 to 26
Outputs:
- newton_step: float32 [16, 2048, 604], P('feat', 'dp')
- residual: float32 [16, 2048, 604], P('feat', 'dp')
Inputs may be any that keep to these rules, and one draw needn't show every extreme that they name: `sample_ids`: each entry names a row of its own aligned block of 512 rows of fisher, counted from the block's start; rows may repeat.
All inputs are finite; a program needn't handle non-finite values. No bound on the sum of `labels` on one device may be relied on, other than what follows from the above.
Results may differ from a plain program's by a relative error of at most 0.0005.
Values sent between devices are 32-bit elements; how exact they have to be, the bound alone decides.
No kernel may reach another device: no remote copies, remote signals or barrier semaphores. Data moves between devices by JAX's collectives and lax.ppermute only.
A program may use at most 64 MiB of HBM per device.

v0:
```python
import jax
import jax.numpy as jnp
from jax import lax
from jax.sharding import PartitionSpec as P

ITERS = 3


PENALTY = 8.0


def squared_norm(vector):
    return lax.psum(jnp.sum(vector * vector, axis=0), ("dp", "feat"))


def shards(fisher, sample_ids, labels, weights):
    picked = jnp.take(fisher, sample_ids, axis=0)
    sample_count = picked.shape[0]
    feat_width = picked.shape[1]
    dp_count = lax.axis_size("dp")
    share_width = feat_width // dp_count
    own_first = lax.axis_index("dp") * share_width
    label_sign = 2.0 * labels.astype(jnp.float32) - 1.0
    highest = lax.Precision.HIGHEST

    def weigh(partial_value, scaler):
        summed = lax.psum(partial_value, "feat")
        return scaler(summed, 0, sample_count)

    def transposed(values):
        columns = picked.astype(jnp.float32)
        return lax.psum_scatter(
            lax.dot_general(
                columns,
                values,
                (((0,), (0,)), ((), ())),
                precision=highest,
                preferred_element_type=jnp.float32,
            ),
            "dp",
            scatter_dimension=0,
            tiled=True,
        )

    def loss_scaler(summed, first_row, share_rows):
        fit = jax.nn.sigmoid(label_sign * summed)
        loss_weight = PENALTY * (fit - 1.0) * label_sign
        return (loss_weight, PENALTY * fit * (1.0 - fit))

    first_margins = jnp.dot(picked, weights, preferred_element_type=jnp.float32)
    own_weights = lax.dynamic_slice_in_dim(weights, own_first, share_width, 0).astype(jnp.float32)
    loss_weight, curv_held = weigh(first_margins, loss_scaler)
    gradient = own_weights + transposed(loss_weight)

    def curve_scaler(summed, first_row, share_rows):
        return (curv_held * summed, None)

    newton_step = jnp.zeros_like(gradient)
    residual = -gradient
    direction = residual
    norm_now = squared_norm(residual)
    for iteration in range(ITERS):
        accumulate_columns = picked.astype(jnp.float32)
        product = jnp.dot(
            accumulate_columns,
            lax.all_gather(direction, "dp", axis=0, tiled=True),
            precision=highest,
            preferred_element_type=jnp.float32,
        )
        scaled, unused = weigh(product, curve_scaler)
        image = direction + transposed(scaled)
        along = lax.psum(jnp.sum(direction * image, axis=0), ("dp", "feat"))
        alpha = norm_now / along
        newton_step = newton_step + alpha * direction
        residual = residual - alpha * image
        norm_next = squared_norm(residual)
        direction = residual + norm_next / norm_now * direction
        norm_now = norm_next
    return (newton_step[None], residual[None])


def solution(mesh):
    return jax.shard_map(
        shards,
        mesh=mesh,
        in_specs=(P("dp", "feat"), P("dp"), P("dp", None), P("feat", None)),
        out_specs=(P("feat", "dp", None), P("feat", "dp", None)),
        check_vma=False,
    )
```

profile of v0, /device:TPU:0, one launch (start us, length us, event | category | flops | bytes accessed | tf_op | source)
XLA Modules:
  0.0 1731.7 jit_solution(1209231092252043416)
XLA Ops:
  8.8 3.3 gather_fusion
  12.1 4.9 fusion.32
  17.1 143.9 %all-reduce.6.cloned.1.call-done = f32[512,604]{0,1:T(8,128)} async-done(((f32[512,604]{0,1:T(8,128)}), f32[512,604]{0,1:T(8,128)}) %all-reduce.6.cloned.1.call-update) | async-done | bytes 1237008 | tf_op jit(solution)/shard_map/psum | solution.py:27
  161.0 9.0 fusion.6
  170.1 106.4 %reduce-scatter.5.cloned.1.call-done = f32[256,604]{0,1:T(8,128)} async-done(((f32[2048,604]{0,1:T(8,128)}), f32[256,604]{0,1:T(8,128)}) %reduce-scatter.5.cloned.1.call-update) | async-done | bytes 618512 | tf_op jit(solution)/shard_map/reduce_scatter | solution.py:32
  276.4 2.1 multiply_reduce_fusion.5
  278.6 105.6 %all-gather.4.cloned.1.call-done = f32[2048,604]{0,1:T(8,128)} async-done(((f32[256,604]{0,1:T(8,128)}), f32[2048,604]{0,1:T(8,128)}) %all-gather.4.cloned.1.call-update) | async-done | bytes 4947984 | tf_op jit(solution)/shard_map/all_gather | solution.py:66
  384.2 8.2 fusion.31
  392.9 141.4 %all-reduce.8.cloned.1.call-done = f32[512,604]{0,1:T(8,128)} async-done(((f32[512,604]{0,1:T(8,128)}), f32[512,604]{0,1:T(8,128)}) %all-reduce.8.cloned.1.call-update) | async-done | bytes 1237008 | tf_op jit(solution)/shard_map/psum | solution.py:27
  534.3 9.4 fusion.4
  543.8 106.4 %reduce-scatter.7.cloned.1.call-done = f32[256,604]{0,1:T(8,128)} async-done(((f32[2048,604]{0,1:T(8,128)}), f32[256,604]{0,1:T(8,128)}) %reduce-scatter.7.cloned.1.call-update) | async-done | bytes 618512 | tf_op jit(solution)/shard_map/reduce_scatter | solution.py:32
  651.5 65.6 %all-reduce = (f32[604]{0:T(1024)S(1)}, f32[604]{0:T(1024)S(1)}) all-reduce(f32[604]{0:T(1024)S(1)} %get-tuple-element.14, f32[604]{0:T(1024)S(1)} %get-tuple-element.12), channel_id=1, replica_groups=mesh['dp'=8,'feat'=16] {'dp','feat'}, use_global_device_ids=true, to_apply=%region_3.4 | all-reduce | flops 1208 | bytes 9664 | tf_op jit(solution)/shard_map/psum | solution.py:13
  717.4 62.7 %psum.74 = f32[604]{0:T(1024)S(1)} all-reduce(f32[604]{0:T(1024)S(1)} %multiply_reduce_fusion.3), channel_id=1, replica_groups=mesh['dp'=8,'feat'=16] {'dp','feat'}, use_global_device_ids=true, to_apply=%region_9.10 | all-reduce | flops 604 | bytes 4832 | tf_op jit(solution)/shard_map/psum | solution.py:13
  781.2 102.4 %all-gather.6.cloned.1.call-done = f32[2048,604]{0,1:T(8,128)} async-done(((f32[256,604]{0,1:T(8,128)}), f32[2048,604]{0,1:T(8,128)}) %all-gather.6.cloned.1.call-update) | async-done | bytes 4947984 | tf_op jit(solution)/shard_map/all_gather | solution.py:66
  883.6 8.3 fusion.30
  892.1 141.7 %all-reduce.10.cloned.1.call-done = f32[512,604]{0,1:T(8,128)} async-done(((f32[512,604]{0,1:T(8,128)}), f32[512,604]{0,1:T(8,128)}) %all-reduce.10.cloned.1.call-update) | async-done | bytes 1237008 | tf_op jit(solution)/shard_map/psum | solution.py:27
  1033.8 9.4 fusion.2
  1043.3 106.4 %reduce-scatter.9.cloned.1.call-done = f32[256,604]{0,1:T(8,128)} async-done(((f32[2048,604]{0,1:T(8,128)}), f32[256,604]{0,1:T(8,128)}) %reduce-scatter.9.cloned.1.call-update) | async-done | bytes 618512 | tf_op jit(solution)/shard_map/reduce_scatter | solution.py:32
  1149.7 2.0 multiply_reduce_fusion.2
  1151.7 65.4 %psum.76 = f32[604]{0:T(1024)S(1)} all-reduce(f32[604]{0:T(1024)S(1)} %get-tuple-element.10), channel_id=1, replica_groups=mesh['dp'=8,'feat'=16] {'dp','feat'}, use_global_device_ids=true, to_apply=%region_13.14 | all-reduce | flops 604 | bytes 4832 | tf_op jit(solution)/shard_map/psum | solution.py:72
  1217.1 2.3 multiply_reduce_fusion.1
  1219.4 62.6 %psum.77 = f32[604]{0:T(1024)S(1)} all-reduce(f32[604]{0:T(1024)S(1)} %get-tuple-element.8), channel_id=1, replica_groups=mesh['dp'=8,'feat'=16] {'dp','feat'}, use_global_device_ids=true, to_apply=%region_15.16 | all-reduce | flops 604 | bytes 4832 | tf_op jit(solution)/shard_map/psum | solution.py:13
  1282.0 2.1 multiply_add_fusion.2
  1284.2 102.4 %all-gather.8.cloned.1.call-done = f32[2048,604]{0,1:T(8,128)} async-done(((f32[256,604]{0,1:T(8,128)}), f32[2048,604]{0,1:T(8,128)}) %all-gather.8.cloned.1.call-update) | async-done | bytes 4947984 | tf_op jit(solution)/shard_map/all_gather | solution.py:66
  1386.6 8.3 fusion.29
  1395.1 141.7 %all-reduce.12.cloned.1.call-done = f32[512,604]{0,1:T(8,128)} async-done(((f32[512,604]{0,1:T(8,128)}), f32[512,604]{0,1:T(8,128)}) %all-reduce.12.cloned.1.call-update) | async-done | bytes 1237008 | tf_op jit(solution)/shard_map/psum | solution.py:27
  1536.8 9.4 fusion
  1546.3 106.4 %reduce-scatter.11.cloned.1.call-done = f32[256,604]{0,1:T(8,128)} async-done(((f32[2048,604]{0,1:T(8,128)}), f32[256,604]{0,1:T(8,128)}) %reduce-scatter.11.cloned.1.call-update) | async-done | bytes 618512 | tf_op jit(solution)/shard_map/reduce_scatter | solution.py:32
  1652.7 2.2 multiply_reduce_fusion
  1654.8 65.4 %psum.79 = f32[604]{0:T(1024)S(1)} all-reduce(f32[604]{0:T(1024)S(1)} %get-tuple-element.6), channel_id=1, replica_groups=mesh['dp'=8,'feat'=16] {'dp','feat'}, use_global_device_ids=true, to_apply=%region_19.20 | all-reduce | flops 604 | bytes 4832 | tf_op jit(solution)/shard_map/psum | solution.py:72
  1720.2 1.8 subtract_bitcast_fusion
  1722.0 1.5 copy.7
  (42 shorter events, 7.1 us)
Async XLA Ops:
  7.2 1.6 copy-start
  7.2 153.8 %all-reduce.6.cloned.1.call-start = ((), (), s32[]{:S(2)}) async-start(), calls=%async_computation.4 | async-start | bytes 2490368 | tf_op jit(solution)/shard_map/psum | solution.py:27
  17.1 259.4 %reduce-scatter.5.cloned.1.call-start = ((), (), s32[]{:S(2)}) async-start(), calls=%async_computation.5 | async-start | bytes 5603328 | tf_op jit(solution)/shard_map/reduce_scatter | solution.py:32
  170.0 214.1 %all-gather.4.cloned.1.call-start = ((), (), s32[]{:S(2)}) async-start(), calls=%async_computation.6 | async-start | bytes 5603328 | tf_op jit(solution)/shard_map/all_gather | solution.py:66
  278.5 255.8 %all-reduce.8.cloned.1.call-start = ((), (), s32[]{:S(2)}) async-start(), calls=%async_computation.7 | async-start | bytes 2490368 | tf_op jit(solution)/shard_map/psum | solution.py:27
  392.4 257.8 %reduce-scatter.7.cloned.1.call-start = ((), (), s32[]{:S(2)}) async-start(), calls=%async_computation.8 | async-start | bytes 5603328 | tf_op jit(solution)/shard_map/reduce_scatter | solution.py:32
  543.8 106.4 %copy-start.1 = (f32[256,604]{0,1:T(8,128)S(1)}, f32[256,604]{0,1:T(8,128)}, u32[]{:S(2)}) copy-start(f32[256,604]{0,1:T(8,128)} %get-tuple-element.15) | copy-start | bytes 1855492
  543.8 339.8 %all-gather.6.cloned.1.call-start = ((), (), s32[]{:S(2)}) async-start(), calls=%async_computation.9 | async-start | bytes 5603328 | tf_op jit(solution)/shard_map/all_gather | solution.py:66
  651.5 129.7 %copy-start.3 = (f32[256,604]{0,1:T(8,128)}, f32[256,604]{0,1:T(8,128)S(1)}, u32[]{:S(2)}) copy-start(f32[256,604]{0,1:T(8,128)S(1)} %get-tuple-element.13) | copy-start | bytes 1855492
  781.2 252.6 %all-reduce.10.cloned.1.call-start = ((), (), s32[]{:S(2)}) async-start(), calls=%async_computation.10 | async-start | bytes 2490368 | tf_op jit(solution)/shard_map/psum | solution.py:27
  891.9 257.8 %reduce-scatter.9.cloned.1.call-start = ((), (), s32[]{:S(2)}) async-start(), calls=%async_computation.11 | async-start | bytes 5603328 | tf_op jit(solution)/shard_map/reduce_scatter | solution.py:32
  1043.2 106.4 %copy-start.2 = (f32[256,604]{0,1:T(8,128)S(1)}, f32[256,604]{0,1:T(8,128)}, u32[]{:S(2)}) copy-start(f32[256,604]{0,1:T(8,128)} %multiply_add_fusion.3) | copy-start | bytes 1855492
  1043.3 343.3 %all-gather.8.cloned.1.call-start = ((), (), s32[]{:S(2)}) async-start(), calls=%async_computation.12 | async-start | bytes 5603328 | tf_op jit(solution)/shard_map/all_gather | solution.py:66
  1284.1 252.7 %all-reduce.12.cloned.1.call-start = ((), (), s32[]{:S(2)}) async-start(), calls=%async_computation.13 | async-start | bytes 2490368 | tf_op jit(solution)/shard_map/psum | solution.py:27
  1394.9 257.8 %reduce-scatter.11.cloned.1.call-start = ((), (), s32[]{:S(2)}) async-start(), calls=%async_computation.14 | async-start | bytes 5603328 | tf_op jit(solution)/shard_map/reduce_scatter | solution.py:32
Sparse Core Ops, SparseCore 0:
  17.2 143.7 all-reduce.5
  170.1 106.2 reduce-scatter.4
  278.6 105.4 all-gather.3
  392.5 141.7 all-reduce.7
  543.9 106.2 reduce-scatter.6
  781.3 102.2 all-gather.5
  892.0 141.7 all-reduce.9
  1043.4 106.2 reduce-scatter.8
  1284.2 102.3 all-gather.7
  1395.0 141.7 all-reduce.11
  1546.4 106.2 reduce-scatter.10
where the time goes:
time: 1740 us; the launch traced here: 1730 us
  waiting for transfers between devices  1300 us (75%)
  blocking collectives  322 us (19%)
  matrix products  67 us (4%)
    psum x4, waiting for transfers between devices, weigh(): summed = lax.psum(partial_value, 'feat')  569 us
    reduce_scatter x4, waiting for transfers between devices, transposed(): lax.psum_scatter(lax.dot_general(columns, values, (((0,), (0,)), ((), ())...  425 us
    all_gather x3, waiting for transfers between devices, shards(): lax.all_gather(direction, 'dp', axis=0, tiled=True)  310 us
    psum x3, blocking collectives, squared_norm(): return lax.psum(jnp.sum(vector * vector, axis=0), ('dp', 'feat'))  191 us
    psum x2, blocking collectives, shards(): along = lax.psum(jnp.sum(direction * image, axis=0), ('dp', 'feat'))  131 us
    dot_general x4, matrix products, transposed(): lax.dot_general(columns, values, (((0,), (0,)), ((), ())), precision=high...  37.3 us
  transfers between devices with their start and end apart: 11, of which 11 were waited for; matrix products, arithmetic and copies ran while one was open for 0% of the time, Pallas kernels for 0%

commit v1 on v0

v1 whole, which is shorter than its diff:
```python
import jax
import jax.numpy as jnp
from jax import lax
from jax.sharding import PartitionSpec as P

ITERS = 3
PENALTY = 8.0
NY, NX, NZ, NH, NC = 4, 2, 4, 2, 2
CHUNKS = 4
PIECE = 32


def dp_move(value, dy, dx=0):
    pairs = [(y * NX + x, ((y + dy) % NY) * NX + (x + dx) % NX) for y in range(NY) for x in range(NX)]
    return lax.ppermute(value, "dp", pairs)


def feat_move(value, dz, dh, dc):
    pairs = [
        ((z * NH + h) * NC + c, (((z + dz) % NZ) * NH + (h + dh) % NH) * NC + (c + dc) % NC)
        for z in range(NZ) for h in range(NH) for c in range(NC)
    ]
    return lax.ppermute(value, "feat", pairs)


def core_swap(value):
    return feat_move(value, 0, 0, 1)


OFFSETS = [(dz, dh) for dz in range(NZ) for dh in range(NH)]


def halves(value):
    high = lax.reduce_precision(value, 8, 7)
    return jnp.concatenate([high.astype(jnp.bfloat16), (value - high).astype(jnp.bfloat16)], axis=0)


def product(value, matrix, dim):
    both = lax.dot_general(halves(value), matrix, (((1,), (dim,)), ((), ())), preferred_element_type=jnp.float32)
    count = value.shape[0]
    return both[:count] + both[count:]


def to_tile(vectors):
    rows = [jnp.pad(v, (0, 256 - v.shape[0])).reshape(2, 128) for v in vectors]
    tile = jnp.concatenate(rows, axis=0)
    return jnp.pad(tile, ((0, 8 - tile.shape[0]), (0, 0)))


def from_tile(tile, place, count):
    return tile[2 * place:2 * place + 2].reshape(256)[:count]


def shards(fisher, sample_ids, labels, weights):
    dp = lax.axis_index("dp")
    feat = lax.axis_index("feat")
    y, x = dp // NX, dp % NX
    z, h, c = feat // (NH * NC), (feat // NC) % NH, feat % NC
    rows, width = fisher.shape
    classes = labels.shape[1]
    group = classes // NY
    held = group + (-group) % 8
    chunk = width // CHUNKS

    ids = sample_ids.reshape(NC, NZ, NH, PIECE)
    ids = jnp.where(c == 1, ids[::-1], ids)
    ids = lax.dynamic_slice_in_dim(jnp.concatenate([ids, ids], axis=1), z, NZ, 1)
    ids = jnp.where(h == 1, ids[:, :, ::-1], ids)
    picked = jnp.take(fisher, ids.reshape(rows), axis=0, mode="clip")

    blocks = []
    half = rows // 2
    for k in range(CHUNKS):
        with jax.named_scope("rows_along_y"):
            own = picked[:, k * chunk:(k + 1) * chunk]
            wide = 2.0 * own.astype(jnp.float32)
            before = dp_move(wide, 1)
            after = dp_move(wide, -1)
            far_a = dp_move(before[:half], 1)
            far_b = dp_move(after[half:], -1)
            far = jnp.concatenate([far_a, far_b], axis=0)
            slots = [own] + [(0.5 * v).astype(jnp.bfloat16) for v in (before, far, after)]
            pieces = [v.reshape(NC * NZ * NH, 1, PIECE, chunk) for v in slots]
            blocks.append(jnp.concatenate(pieces, axis=1).reshape(NY * rows, chunk))

    with jax.named_scope("margins"):
        partial = jnp.dot(picked, weights, preferred_element_type=jnp.float32)
        partial = partial[:half] + core_swap(partial[half:])
        summed = partial[:PIECE]
        for place, (dz, dh) in enumerate(OFFSETS):
            if place:
                summed = summed + feat_move(partial[place * PIECE:(place + 1) * PIECE], dz, dh, 0)
        own_labels = lax.dynamic_slice_in_dim(labels, ((c * NZ + z) * NH + h) * PIECE, PIECE, 0)
        label_sign = 2.0 * own_labels.astype(jnp.float32) - 1.0
        fit = jax.nn.sigmoid(label_sign * summed)
        loss_weight = PENALTY * (fit - 1.0) * label_sign
        curv = PENALTY * fit * (1.0 - fit)
        both = jnp.stack([loss_weight, curv]).reshape(2, PIECE, NY, group).transpose(2, 0, 3, 1)
        both = jnp.pad(both, ((0, 0), (0, 0), (0, held - group), (0, 0)))
        slots = []
        for k in range(NY):
            part = lax.dynamic_index_in_dim(both, (y + k) % NY, 0, keepdims=False)
            slots.append(part if k == 0 else dp_move(part, k))
        both = jnp.concatenate(slots, axis=2)
        loss_share, curv_share = both[0], both[1]

    def spread(share, tile):
        got = share if tile is None else jnp.concatenate([share, tile], axis=0)
        parts = [got] + [feat_move(got, -dz, -dh, 0) for dz, dh in OFFSETS[1:]]
        near = jnp.concatenate([v[:held] for v in parts], axis=1)
        whole = jnp.concatenate([near, core_swap(near)], axis=1)
        if tile is None:
            return whole, None
        total = parts[0][held:]
        for v in parts[1:]:
            total = total + v[held:]
        return whole, total + core_swap(total)

    def reduce(partial, tile):
        mid = partial.shape[1] // 2
        near = partial[:, :mid] + core_swap(partial[:, mid:])
        tile = tile + core_swap(tile)
        total = None
        for place, (dz, dh) in enumerate(OFFSETS):
            sent = jnp.concatenate([near[:, place * 128:(place + 1) * 128], tile], axis=0)
            got = sent if place == 0 else feat_move(sent, dz, dh, 0)
            total = got if total is None else total + got
        return total[:held], total[held:]

    with jax.named_scope("loss_spread"):
        loss_all, _ = spread(loss_share, None)

    own_weights = lax.dynamic_slice_in_dim(weights, y * group, group, 1).astype(jnp.float32).T
    own_weights = jnp.pad(own_weights, ((0, held - group), (0, 0)))

    residual = []
    partial, norm = 0.0, 0.0
    for k in range(CHUNKS):
        with jax.named_scope("gradient"):
            back = product(loss_all, blocks[k], 0)
            back = back + dp_move(back, 0, 1)
            value = -(own_weights[:, k * chunk:(k + 1) * chunk] + back)
            residual.append(value)
            norm = norm + jnp.sum(value * value, axis=1)
            partial = partial + product(value, blocks[k], 1)

    step = [0.0] * CHUNKS
    direction = swing = norm_now = None
    for iteration in range(ITERS):
        with jax.named_scope("sum_over_features"):
            mapped, tile = reduce(partial, to_tile([norm]))
            norm_next = from_tile(tile, 0, held)
        if iteration == 0:
            direction, swing = list(residual), mapped
        else:
            beta = (norm_next / norm_now)[:, None]
            direction = [r + beta * d for r, d in zip(residual, direction)]
            swing = mapped + beta * swing
        norm_now = norm_next
        with jax.named_scope("spread_scaled"):
            scaled = curv_share * swing
            curved = jnp.sum(scaled * swing, axis=1)
            plain = sum(jnp.sum(d * d, axis=1) for d in direction)
            scaled_all, tile = spread(scaled, to_tile([curved, plain]))
            curved = from_tile(tile, 0, held)
            curved = curved + dp_move(curved, 0, 1)
            alpha = (norm_now / (from_tile(tile, 1, held) + curved))[:, None]
        step = [n + alpha * d for n, d in zip(step, direction)]
        last = iteration == ITERS - 1
        partial, norm = 0.0, 0.0
        for k in range(CHUNKS):
            with jax.named_scope("image"):
                back = product(scaled_all, blocks[k], 0)
                if last:
                    share = chunk // NX
                    sent = lax.dynamic_slice_in_dim(back, (1 - x) * share, share, 1)
                    kept = lax.dynamic_slice_in_dim(back, x * share, share, 1)
                    image = lax.dynamic_slice_in_dim(direction[k], x * share, share, 1) + (kept + dp_move(sent, 0, 1))
                    residual[k] = lax.dynamic_slice_in_dim(residual[k], x * share, share, 1) - alpha * image
                    step[k] = lax.dynamic_slice_in_dim(step[k], x * share, share, 1)
                else:
                    image = direction[k] + (back + dp_move(back, 0, 1))
                    residual[k] = residual[k] - alpha * image
                    norm = norm + jnp.sum(residual[k] * residual[k], axis=1)
                    partial = partial + product(residual[k], blocks[k], 1)

    def place_out(parts):
        stacked = jnp.stack(parts)
        slots = []
        for k in range(NY):
            part = lax.dynamic_index_in_dim(stacked, (y + k) % NY, 0, keepdims=False)
            slots.append(part if k == 0 else dp_move(part, k))
        slots = jnp.stack(slots)
        ordered = [lax.dynamic_index_in_dim(slots, (y - g) % NY, 0, keepdims=False)[:group] for g in range(NY)]
        return jnp.concatenate(ordered, axis=0).T[None]

    with jax.named_scope("outputs"):
        return place_out(step), place_out(residual)


def solution(mesh):
    return jax.shard_map(
        shards,
        mesh=mesh,
        in_specs=(P("dp", "feat"), P("dp"), P("dp", None), P("feat", None)),
        out_specs=(P("feat", "dp", None), P("feat", "dp", None)),
        check_vma=False,
    )
```

time: 1740 us -> 489 us (0.28)
  waiting for transfers between devices: 1300 us -> 212 us
  blocking collectives: 322 us -> 0 us
  starting transfers between devices: 1.31 us -> 176 us
  matrix products: 67 us -> 26.1 us
  local copies, waits for them, and re-layouts: 6.31 us -> 39.1 us
    psum x4 -> x0, waiting for transfers between devices: 569 us -> none  [weigh(): summed = lax.psum(partial_value, 'feat')]
    reduce_scatter x4 -> x0, waiting for transfers between devices: 425 us -> none  [transposed(): lax.psum_scatter(lax.dot_general(columns, values, (((0,), (0,)), ((), ())...]
    psum x5 -> x0, blocking collectives: 322 us -> none  [the longest x3 191 us: squared_norm(): return lax.psum(jnp.sum(vector * vector, axis=0), ('dp', 'feat'))]
    all_gather x3 -> x0, waiting for transfers between devices: 310 us -> none  [shards(): lax.all_gather(direction, 'dp', axis=0, tiled=True)]
    ppermute x0 -> x114, waiting for transfers between devices: none -> 212 us  [the longest x44 144 us: dp_move(): return lax.ppermute(value, 'dp', pairs)]
    ppermute x0 -> x114, starting transfers between devices: none -> 176 us  [the longest x70 117 us: feat_move(): return lax.ppermute(value, 'feat', pairs)]
    dot_general x8 -> x29, matrix products: 67 us -> 26.1 us  [the longest x28 23 us: product(): lax.dot_general(halves(value), matrix, (((1,), (dim,)), ((), ())), prefer...]
  transfers between devices with their start and end apart: 11 -> 114, of which waited for: 11 -> 58; matrix products, arithmetic and copies ran while one was open for 0% -> 8% of each run, Pallas kernels for 0% -> 0%
where the time goes in v1:
time: 489 us; the launch traced here: 479 us
  waiting for transfers between devices  212 us (43%)
  starting transfers between devices  176 us (36%)
  local copies, waits for them, and re-layouts  39.1 us (8%)
  matrix products  26.1 us (5%)
  other arithmetic  23.2 us (5%)
    ppermute x44, waiting for transfers between devices, dp_move(): return lax.ppermute(value, 'dp', pairs)  144 us
    ppermute x70, starting transfers between devices, feat_move(): return lax.ppermute(value, 'feat', pairs)  117 us
    ppermute x70, waiting for transfers between devices, feat_move(): return lax.ppermute(value, 'feat', pairs)  68.1 us
    ppermute x44, starting transfers between devices, dp_move(): return lax.ppermute(value, 'dp', pairs)  59 us
    dot_general x28, matrix products, product(): lax.dot_general(halves(value), matrix, (((1,), (dim,)), ((), ())), prefer...  23 us
    unnamed x100, local copies, waits for them, and re-layouts  11.7 us
  transfers between devices with their start and end apart: 114, of which 58 were waited for; matrix products, arithmetic and copies ran while one was open for 8% of the time, Pallas kernels for 0%

profile of v1, /device:TPU:0, one launch (start us, length us, event | category | flops | bytes accessed | tf_op | source)
XLA Modules:
  0.0 479.4 jit_solution(1747811674534718391)
XLA Ops:
  1.8 7.1 %gather_fusion = bf16[512,2048]{1,0:T(8,128)(2,1)} fusion(bf16[512,2048]{1,0:T(8,128)(2,1)} %param.4, s32[1024]{0:T(1024)S(1)} %pad_clamp_fusion), kind=kCustom, calls=%fused_computation | custom fusion | bytes 4196352 | tf_op jit(solution)/shard_map/jit(_take)/gather | solution.py:69
  19.8 6.6 %collective-permute-start.7 = (f32[32,604]{1,0:T(8,128)S(1)}, f32[32,604]{1,0:T(8,128)S(1)}, u32[]{:S(2)}, u32[]{:S(2)}) collective-permute-start(f32[32,604]{1,0:T(8,128)S(1)} %get-tuple-element.92), channel_id=1, source_target_pairs={{0,14},{1,15},{2,12},{3,13},{4,2},{5,3},{6,0},{7,1},{8,6},{9,7},{1... | collective-permute-start | bytes 231944 | tf_op jit(solution)/shard_map/margins/ppermute | solution.py:23
  29.0 3.5 collective-permute-start.4
  32.5 4.1 collective-permute-start.3
  57.3 13.0 %collective-permute-done.10 = f32[2,152,32]{2,1,0:T(8,128)} collective-permute-done((f32[2,152,32]{2,1,0:T(8,128)}, f32[2,152,32]{2,1,0:T(8,128)}, u32[]{:S(2)}, u32[]{:S(2)}) %collective-permute-start.10) | collective-permute-done | bytes 38944 | tf_op jit(solution)/shard_map/margins/ppermute | solution.py:15
  70.2 3.7 collective-permute-start.21
  87.3 6.1 %collective-permute-start.13 = (f32[152,128]{1,0:T(8,128)S(1)}, f32[152,128]{1,0:T(8,128)S(1)}, u32[]{:S(2)}, u32[]{:S(2)}) collective-permute-start(f32[152,128]{1,0:T(8,128)S(1)} %slice_bitcast_fusion.1), channel_id=1, source_target_pairs={{0,14},{1,15},{2,12},{3,13},{4,2},{5,3},{6,0},{7,1},{8,6},{9,7},{1... | collective-permute-start | bytes 233480 | tf_op jit(solution)/shard_map/loss_spread/ppermute | solution.py:23
  97.3 4.3 collective-permute-done.14
  103.9 6.2 %collective-permute-done.15 = f32[152,128]{1,0:T(8,128)S(1)} collective-permute-done((f32[152,128]{1,0:T(8,128)S(1)}, f32[152,128]{1,0:T(8,128)S(1)}, u32[]{:S(2)}, u32[]{:S(2)}) %collective-permute-start.15) | collective-permute-done | bytes 77856 | tf_op jit(solution)/shard_map/loss_spread/ppermute | solution.py:23
  111.3 4.4 collective-permute-done.16
  118.0 5.7 %collective-permute-done.17 = f32[152,128]{1,0:T(8,128)S(1)} collective-permute-done((f32[152,128]{1,0:T(8,128)S(1)}, f32[152,128]{1,0:T(8,128)S(1)}, u32[]{:S(2)}, u32[]{:S(2)}) %collective-permute-start.17) | collective-permute-done | bytes 77856 | tf_op jit(solution)/shard_map/loss_spread/ppermute | solution.py:23
  135.7 14.9 %collective-permute-done.31 = f32[512,512]{1,0:T(8,128)S(1)} collective-permute-done((f32[512,512]{1,0:T(8,128)S(1)}, f32[512,512]{1,0:T(8,128)S(1)}, u32[]{:S(2)}, u32[]{:S(2)}) %collective-permute-start.31) | collective-permute-done | bytes 1048608 | tf_op jit(solution)/shard_map/rows_along_y/ppermute | solution.py:15
  150.6 3.7 collective-permute-start.37
  154.8 18.3 %collective-permute-done.26 = f32[512,512]{1,0:T(8,128)S(1)} collective-permute-done((f32[512,512]{1,0:T(8,128)S(1)}, f32[512,512]{1,0:T(8,128)S(1)}, u32[]{:S(2)}, u32[]{:S(2)}) %collective-permute-start.26) | collective-permute-done | bytes 1048608 | tf_op jit(solution)/shard_map/rows_along_y/ppermute | solution.py:15
  173.1 3.7 collective-permute-start.22
  180.8 11.7 %collective-permute-done.22 = f32[256,512]{1,0:T(8,128)S(1)} collective-permute-done((f32[256,512]{1,0:T(8,128)S(1)}, f32[256,512]{1,0:T(8,128)S(1)}, u32[]{:S(2)}, u32[]{:S(2)}) %collective-permute-start.22) | collective-permute-done | bytes 524320 | tf_op jit(solution)/shard_map/rows_along_y/ppermute | solution.py:15
  192.6 3.4 collective-permute-done.20
  199.4 3.9 collective-permute-done.30
  213.6 3.3 collective-permute-done.38
  216.9 3.3 collective-permute-done.28
  230.6 3.7 collective-permute-start.45
  234.2 4.2 collective-permute-start.43
  276.3 5.8 %collective-permute-done.59 = f32[152,512]{1,0:T(8,128)S(1)} collective-permute-done((f32[152,512]{1,0:T(8,128)S(1)}, f32[152,512]{1,0:T(8,128)S(1)}, u32[]{:S(2)}, u32[]{:S(2)}) %collective-permute-start.59) | collective-permute-done | bytes 311328 | tf_op jit(solution)/shard_map/image/ppermute | solution.py:15
  282.1 6.7 %collective-permute-done.58 = f32[152,512]{1,0:T(8,128)S(1)} collective-permute-done((f32[152,512]{1,0:T(8,128)S(1)}, f32[152,512]{1,0:T(8,128)S(1)}, u32[]{:S(2)}, u32[]{:S(2)}) %collective-permute-start.58) | collective-permute-done | bytes 311328 | tf_op jit(solution)/shard_map/image/ppermute | solution.py:15
  288.8 6.7 %collective-permute-done.60 = f32[152,512]{1,0:T(8,128)S(1)} collective-permute-done((f32[152,512]{1,0:T(8,128)S(1)}, f32[152,512]{1,0:T(8,128)S(1)}, u32[]{:S(2)}, u32[]{:S(2)}) %collective-permute-start.60) | collective-permute-done | bytes 311328 | tf_op jit(solution)/shard_map/image/ppermute | solution.py:15
  295.5 5.6 %collective-permute-done.61 = f32[152,512]{1,0:T(8,128)S(1)} collective-permute-done((f32[152,512]{1,0:T(8,128)S(1)}, f32[152,512]{1,0:T(8,128)S(1)}, u32[]{:S(2)}, u32[]{:S(2)}) %collective-permute-start.61) | collective-permute-done | bytes 311328 | tf_op jit(solution)/shard_map/image/ppermute | solution.py:15
  311.8 3.8 collective-permute-start.68
  315.7 4.1 collective-permute-start.66
  357.9 24.2 %collective-permute-done.79 = f32[152]{0:T(256)S(1)} collective-permute-done((f32[152]{0:T(256)S(1)}, f32[152]{0:T(256)S(1)}, u32[]{:S(2)}, u32[]{:S(2)}) %collective-permute-start.79) | collective-permute-done | bytes 640 | tf_op jit(solution)/shard_map/spread_scaled/ppermute | solution.py:15
  393.3 3.8 collective-permute-start.91
  397.0 4.2 collective-permute-start.89
  451.6 3.3 collective-permute-done.107
  (504 shorter events, 269.7 us)
Async XLA Ops:
  19.8 16.8 %collective-permute-start.7 = (f32[32,604]{1,0:T(8,128)S(1)}, f32[32,604]{1,0:T(8,128)S(1)}, u32[]{:S(2)}, u32[]{:S(2)}) collective-permute-start(f32[32,604]{1,0:T(8,128)S(1)} %get-tuple-element.92), channel_id=1, source_target_pairs={{0,14},{1,15},{2,12},{3,13},{4,2},{5,3},{6,0},{7,1},{8,6},{9,7},{1... | collective-permute-start | bytes 231944 | tf_op jit(solution)/shard_map/margins/ppermute | solution.py:23
  29.0 13.2 %collective-permute-start.4 = (f32[32,604]{1,0:T(8,128)}, f32[32,604]{1,0:T(8,128)}, u32[]{:S(2)}, u32[]{:S(2)}) collective-permute-start(f32[32,604]{1,0:T(8,128)} %get-tuple-element.95), channel_id=1, source_target_pairs={{0,8},{1,9},{2,10},{3,11},{4,12},{5,13},{6,14},{7,15},{8,0},{9,1},... | collective-permute-start | bytes 231944 | tf_op jit(solution)/shard_map/margins/ppermute | solution.py:23
  39.1 87.9 %collective-permute-start.36 = (f32[512,512]{1,0:T(8,128)}, f32[512,512]{1,0:T(8,128)}, u32[]{:S(2)}, u32[]{:S(2)}) collective-permute-start(f32[512,512]{1,0:T(8,128)} %get-tuple-element.70), channel_id=1, source_target_pairs={{0,96},{16,112},{32,0},{48,16},{64,32},{80,48},{96,64},{112,80},{1... | collective-permute-start | bytes 3145736 | tf_op jit(solution)/shard_map/rows_along_y/ppermute | solution.py:15
  42.2 86.0 %collective-permute-start.34 = (f32[512,512]{1,0:T(8,128)}, f32[512,512]{1,0:T(8,128)}, u32[]{:S(2)}, u32[]{:S(2)}) collective-permute-start(f32[512,512]{1,0:T(8,128)} %get-tuple-element.70), channel_id=1, source_target_pairs={{0,32},{16,48},{32,64},{48,80},{64,96},{80,112},{96,0},{112,16},{1... | collective-permute-start | bytes 3145736 | tf_op jit(solution)/shard_map/rows_along_y/ppermute | solution.py:15
  46.8 23.4 %collective-permute-start.10 = (f32[2,152,32]{2,1,0:T(8,128)}, f32[2,152,32]{2,1,0:T(8,128)}, u32[]{:S(2)}, u32[]{:S(2)}) collective-permute-start(f32[2,152,32]{2,1,0:T(8,128)} %bitcast.5), channel_id=1, source_target_pairs={{0,96},{16,112},{32,0},{48,16},{64,32},{80,48},{96,64},{112,80},{1... | collective-permute-start | bytes 116744 | tf_op jit(solution)/shard_map/margins/ppermute | solution.py:15
  50.6 23.4 %collective-permute-start.9 = (f32[2,152,32]{2,1,0:T(8,128)}, f32[2,152,32]{2,1,0:T(8,128)}, u32[]{:S(2)}, u32[]{:S(2)}) collective-permute-start(f32[2,152,32]{2,1,0:T(8,128)} %bitcast.4), channel_id=1, source_target_pairs={{0,64},{16,80},{32,96},{48,112},{64,0},{80,16},{96,32},{112,48},{1... | collective-permute-start | bytes 116744 | tf_op jit(solution)/shard_map/margins/ppermute | solution.py:15
  52.0 22.0 %collective-permute-start.8 = (f32[2,152,32]{2,1,0:T(8,128)}, f32[2,152,32]{2,1,0:T(8,128)}, u32[]{:S(2)}, u32[]{:S(2)}) collective-permute-start(f32[2,152,32]{2,1,0:T(8,128)} %bitcast.3), channel_id=1, source_target_pairs={{0,32},{16,48},{32,64},{48,80},{64,96},{80,112},{96,0},{112,16},{1... | collective-permute-start | bytes 116744 | tf_op jit(solution)/shard_map/margins/ppermute | solution.py:15
  70.2 65.0 %collective-permute-start.21 = (f32[512,512]{1,0:T(8,128)}, f32[512,512]{1,0:T(8,128)S(1)}, u32[]{:S(2)}, u32[]{:S(2)}) collective-permute-start(f32[512,512]{1,0:T(8,128)} %get-tuple-element.67), channel_id=1, source_target_pairs={{0,96},{16,112},{32,0},{48,16},{64,32},{80,48},{96,64},{112,80},{1... | collective-permute-start | bytes 3145736 | tf_op jit(solution)/shard_map/rows_along_y/ppermute | solution.py:15
  74.0 61.5 %collective-permute-start.19 = (f32[512,512]{1,0:T(8,128)}, f32[512,512]{1,0:T(8,128)S(1)}, u32[]{:S(2)}, u32[]{:S(2)}) collective-permute-start(f32[512,512]{1,0:T(8,128)} %get-tuple-element.67), channel_id=1, source_target_pairs={{0,32},{16,48},{32,64},{48,80},{64,96},{80,112},{96,0},{112,16},{1... | collective-permute-start | bytes 3145736 | tf_op jit(solution)/shard_map/rows_along_y/ppermute | solution.py:15
  123.7 26.9 %collective-permute-start.31 = (f32[512,512]{1,0:T(8,128)S(1)}, f32[512,512]{1,0:T(8,128)S(1)}, u32[]{:S(2)}, u32[]{:S(2)}) collective-permute-start(f32[512,512]{1,0:T(8,128)S(1)} %copy-done.32), channel_id=1, source_target_pairs={{0,96},{16,112},{32,0},{48,16},{64,32},{80,48},{96,64},{112,80},{1... | collective-permute-start | bytes 3145736 | tf_op jit(solution)/shard_map/rows_along_y/ppermute | solution.py:15
  127.0 27.4 %collective-permute-start.29 = (f32[512,512]{1,0:T(8,128)S(1)}, f32[512,512]{1,0:T(8,128)S(1)}, u32[]{:S(2)}, u32[]{:S(2)}) collective-permute-start(f32[512,512]{1,0:T(8,128)S(1)} %copy-done.32), channel_id=1, source_target_pairs={{0,32},{16,48},{32,64},{48,80},{64,96},{80,112},{96,0},{112,16},{1... | collective-permute-start | bytes 3145736 | tf_op jit(solution)/shard_map/rows_along_y/ppermute | solution.py:15
  128.2 44.9 %collective-permute-start.26 = (f32[512,512]{1,0:T(8,128)S(1)}, f32[512,512]{1,0:T(8,128)S(1)}, u32[]{:S(2)}, u32[]{:S(2)}) collective-permute-start(f32[512,512]{1,0:T(8,128)S(1)} %copy-done.31), channel_id=1, source_target_pairs={{0,96},{16,112},{32,0},{48,16},{64,32},{80,48},{96,64},{112,80},{1... | collective-permute-start | bytes 3145736 | tf_op jit(solution)/shard_map/rows_along_y/ppermute | solution.py:15
  135.3 41.5 %collective-permute-start.24 = (f32[512,512]{1,0:T(8,128)S(1)}, f32[512,512]{1,0:T(8,128)S(1)}, u32[]{:S(2)}, u32[]{:S(2)}) collective-permute-start(f32[512,512]{1,0:T(8,128)S(1)} %copy-done.31), channel_id=1, source_target_pairs={{0,32},{16,48},{32,64},{48,80},{64,96},{80,112},{96,0},{112,16},{1... | collective-permute-start | bytes 3145736 | tf_op jit(solution)/shard_map/rows_along_y/ppermute | solution.py:15
  135.5 41.7 %collective-permute-start.18 = (f32[152,1024]{1,0:T(8,128)S(1)}, f32[152,1024]{1,0:T(8,128)S(1)}, u32[]{:S(2)}, u32[]{:S(2)}) collective-permute-start(f32[152,1024]{1,0:T(8,128)S(1)} %get-tuple-element.216), channel_id=1, source_target_pairs={{0,1},{1,0},{2,3},{3,2},{4,5},{5,4},{6,7},{7,6},{8,9},{9,8},{10,11... | collective-permute-start | bytes 1867784 | tf_op jit(solution)/shard_map/loss_spread/ppermute | solution.py:23
  150.6 55.2 %collective-permute-start.37 = (f32[256,512]{1,0:T(8,128)S(1)}, f32[256,512]{1,0:T(8,128)S(1)}, u32[]{:S(2)}, u32[]{:S(2)}) collective-permute-start(f32[256,512]{1,0:T(8,128)S(1)} %slice.818), channel_id=1, source_target_pairs={{0,96},{16,112},{32,0},{48,16},{64,32},{80,48},{96,64},{112,80},{1... | collective-permute-start | bytes 1572872 | tf_op jit(solution)/shard_map/rows_along_y/ppermute | solution.py:15
  154.4 52.3 %collective-permute-start.35 = (f32[256,512]{1,0:T(8,128)S(1)}, f32[256,512]{1,0:T(8,128)S(1)}, u32[]{:S(2)}, u32[]{:S(2)}) collective-permute-start(f32[256,512]{1,0:T(8,128)S(1)} %slice.817), channel_id=1, source_target_pairs={{0,32},{16,48},{32,64},{48,80},{64,96},{80,112},{96,0},{112,16},{1... | collective-permute-start | bytes 1572872 | tf_op jit(solution)/shard_map/rows_along_y/ppermute | solution.py:15
  173.1 19.4 %collective-permute-start.22 = (f32[256,512]{1,0:T(8,128)S(1)}, f32[256,512]{1,0:T(8,128)S(1)}, u32[]{:S(2)}, u32[]{:S(2)}) collective-permute-start(f32[256,512]{1,0:T(8,128)S(1)} %slice.794), channel_id=1, source_target_pairs={{0,96},{16,112},{32,0},{48,16},{64,32},{80,48},{96,64},{112,80},{1... | collective-permute-start | bytes 1572872 | tf_op jit(solution)/shard_map/rows_along_y/ppermute | solution.py:15
  176.8 19.2 %collective-permute-start.20 = (f32[256,512]{1,0:T(8,128)S(1)}, f32[256,512]{1,0:T(8,128)S(1)}, u32[]{:S(2)}, u32[]{:S(2)}) collective-permute-start(f32[256,512]{1,0:T(8,128)S(1)} %slice.793), channel_id=1, source_target_pairs={{0,32},{16,48},{32,64},{48,80},{64,96},{80,112},{96,0},{112,16},{1... | collective-permute-start | bytes 1572872 | tf_op jit(solution)/shard_map/rows_along_y/ppermute | solution.py:15
  177.2 20.9 %collective-permute-start.32 = (f32[256,512]{1,0:T(8,128)S(1)}, f32[256,512]{1,0:T(8,128)S(1)}, u32[]{:S(2)}, u32[]{:S(2)}) collective-permute-start(f32[256,512]{1,0:T(8,128)S(1)} %slice.810), channel_id=1, source_target_pairs={{0,96},{16,112},{32,0},{48,16},{64,32},{80,48},{96,64},{112,80},{1... | collective-permute-start | bytes 1572872 | tf_op jit(solution)/shard_map/rows_along_y/ppermute | solution.py:15
  196.0 13.7 %collective-permute-start.27 = (f32[256,512]{1,0:T(8,128)S(1)}, f32[256,512]{1,0:T(8,128)S(1)}, u32[]{:S(2)}, u32[]{:S(2)}) collective-permute-start(f32[256,512]{1,0:T(8,128)S(1)} %slice.802), channel_id=1, source_target_pairs={{0,96},{16,112},{32,0},{48,16},{64,32},{80,48},{96,64},{112,80},{1... | collective-permute-start | bytes 1572872 | tf_op jit(solution)/shard_map/rows_along_y/ppermute | solution.py:15
  198.1 11.6 %collective-permute-start.25 = (f32[256,512]{1,0:T(8,128)S(1)}, f32[256,512]{1,0:T(8,128)S(1)}, u32[]{:S(2)}, u32[]{:S(2)}) collective-permute-start(f32[256,512]{1,0:T(8,128)S(1)} %slice.801), channel_id=1, source_target_pairs={{0,32},{16,48},{32,64},{48,80},{64,96},{80,112},{96,0},{112,16},{1... | collective-permute-start | bytes 1572872 | tf_op jit(solution)/shard_map/rows_along_y/ppermute | solution.py:15
  272.8 16.0 %collective-permute-start.58 = (f32[152,512]{1,0:T(8,128)S(1)}, f32[152,512]{1,0:T(8,128)S(1)}, u32[]{:S(2)}, u32[]{:S(2)}) collective-permute-start(f32[152,512]{1,0:T(8,128)S(1)} %slice_add_fusion.26), channel_id=1, source_target_pairs={{0,16},{16,0},{32,48},{48,32},{64,80},{80,64},{96,112},{112,96},{1... | collective-permute-start | bytes 933896 | tf_op jit(solution)/shard_map/image/ppermute | solution.py:15
  274.1 21.4 %collective-permute-start.60 = (f32[152,512]{1,0:T(8,128)S(1)}, f32[152,512]{1,0:T(8,128)S(1)}, u32[]{:S(2)}, u32[]{:S(2)}) collective-permute-start(f32[152,512]{1,0:T(8,128)S(1)} %slice_add_fusion.24), channel_id=1, source_target_pairs={{0,16},{16,0},{32,48},{48,32},{64,80},{80,64},{96,112},{112,96},{1... | collective-permute-start | bytes 933896 | tf_op jit(solution)/shard_map/image/ppermute | solution.py:15
  275.1 25.9 %collective-permute-start.61 = (f32[152,512]{1,0:T(8,128)S(1)}, f32[152,512]{1,0:T(8,128)S(1)}, u32[]{:S(2)}, u32[]{:S(2)}) collective-permute-start(f32[152,512]{1,0:T(8,128)S(1)} %slice_add_fusion.23), channel_id=1, source_target_pairs={{0,16},{16,0},{32,48},{48,32},{64,80},{80,64},{96,112},{112,96},{1... | collective-permute-start | bytes 933896 | tf_op jit(solution)/shard_map/image/ppermute | solution.py:15
  352.5 29.6 %collective-permute-start.82 = (f32[152,512]{1,0:T(8,128)S(1)}, f32[152,512]{1,0:T(8,128)S(1)}, u32[]{:S(2)}, u32[]{:S(2)}) collective-permute-start(f32[152,512]{1,0:T(8,128)S(1)} %slice_add_fusion.21), channel_id=1, source_target_pairs={{0,16},{16,0},{32,48},{48,32},{64,80},{80,64},{96,112},{112,96},{1... | collective-permute-start | bytes 933896 | tf_op jit(solution)/shard_map/image/ppermute | solution.py:15
  353.5 28.6 %collective-permute-start.81 = (f32[152,512]{1,0:T(8,128)S(1)}, f32[152,512]{1,0:T(8,128)S(1)}, u32[]{:S(2)}, u32[]{:S(2)}) collective-permute-start(f32[152,512]{1,0:T(8,128)S(1)} %slice_add_fusion.22), channel_id=1, source_target_pairs={{0,16},{16,0},{32,48},{48,32},{64,80},{80,64},{96,112},{112,96},{1... | collective-permute-start | bytes 933896 | tf_op jit(solution)/shard_map/image/ppermute | solution.py:15
  354.8 27.3 %collective-permute-start.83 = (f32[152,512]{1,0:T(8,128)S(1)}, f32[152,512]{1,0:T(8,128)S(1)}, u32[]{:S(2)}, u32[]{:S(2)}) collective-permute-start(f32[152,512]{1,0:T(8,128)S(1)} %slice_add_fusion.20), channel_id=1, source_target_pairs={{0,16},{16,0},{32,48},{48,32},{64,80},{80,64},{96,112},{112,96},{1... | collective-permute-start | bytes 933896 | tf_op jit(solution)/shard_map/image/ppermute | solution.py:15
  355.8 26.4 %collective-permute-start.84 = (f32[152,512]{1,0:T(8,128)S(1)}, f32[152,512]{1,0:T(8,128)S(1)}, u32[]{:S(2)}, u32[]{:S(2)}) collective-permute-start(f32[152,512]{1,0:T(8,128)S(1)} %slice_add_fusion.19), channel_id=1, source_target_pairs={{0,16},{16,0},{32,48},{48,32},{64,80},{80,64},{96,112},{112,96},{1... | collective-permute-start | bytes 933896 | tf_op jit(solution)/shard_map/image/ppermute | solution.py:15
  357.1 25.0 %collective-permute-start.79 = (f32[152]{0:T(256)S(1)}, f32[152]{0:T(256)S(1)}, u32[]{:S(2)}, u32[]{:S(2)}) collective-permute-start(f32[152]{0:T(256)S(1)} %bitcast.255), channel_id=1, source_target_pairs={{0,16},{16,0},{32,48},{48,32},{64,80},{80,64},{96,112},{112,96},{1... | collective-permute-start | bytes 1832 | tf_op jit(solution)/shard_map/spread_scaled/ppermute | solution.py:15
  413.2 12.2 %collective-permute-start.96 = (f32[160,128]{1,0:T(8,128)S(1)}, f32[160,128]{1,0:T(8,128)S(1)}, u32[]{:S(2)}, u32[]{:S(2)}) collective-permute-start(f32[160,128]{1,0:T(8,128)S(1)} %pad_maximum_fusion.39), channel_id=1, source_target_pairs={{0,14},{1,15},{2,12},{3,13},{4,2},{5,3},{6,0},{7,1},{8,6},{9,7},{1... | collective-permute-start | bytes 245768 | tf_op jit(solution)/shard_map/spread_scaled/ppermute | solution.py:23
  447.9 11.6 %collective-permute-start.108 = (f32[152,256]{1,0:T(8,128)S(1)}, f32[152,256]{1,0:T(8,128)S(1)}, u32[]{:S(2)}, u32[]{:S(2)}) collective-permute-start(f32[152,256]{1,0:T(8,128)S(1)} %constant_dynamic-slice_fusion.3), channel_id=1, source_target_pairs={{0,16},{16,0},{32,48},{48,32},{64,80},{80,64},{96,112},{112,96},{1... | collective-permute-start | bytes 466952 | tf_op jit(solution)/shard_map/image/ppermute | solution.py:15
  463.1 11.5 %collective-permute-start.113 = (f32[152,256]{1,0:T(8,128)S(1)}, f32[152,256]{1,0:T(8,128)S(1)}, u32[]{:S(2)}, u32[]{:S(2)}) collective-permute-start(f32[152,256]{1,0:T(8,128)S(1)} %get-tuple-element.103), channel_id=1, source_target_pairs={{0,96},{16,112},{32,0},{48,16},{64,32},{80,48},{96,64},{112,80},{1... | collective-permute-start | bytes 466952 | tf_op jit(solution)/shard_map/outputs/ppermute | solution.py:15
  (118 other events, 2094.1 us)
